TPU v7x, 32 devices: a whole 2x2x4 slice. The times are simulated.
32 devices in a mesh: grp: 4 (over y, x), col: 8 (over z, core).
Axes of the slice: x: 2, y: 2, z: 4, core: 2. Of those that a mesh axis runs over, the one named last changes fastest.
Arguments:
- orbitals: bfloat16 [2, 6656, 4096], P(None, 'col', 'grp'), may hold values from -6 to 6
- cosine_tiles: bfloat16 [32, 256, 256], P(('grp', 'col')), may hold values from -0.125 to 0.125
- sine_tiles: bfloat16 [32, 256, 256], P(('grp', 'col')), may hold values from -0.125 to 0.125
- tile_row: int32 [32], P('grp'), may hold values from -1 to 3, as said below
- tile_col: int32 [32], P('grp'), may hold values from -1 to 15, as said below
- row_place: int32 [16], replicated, may hold values from 0 to 15, each once
Outputs:
- propagated: bfloat16 [2, 6656, 4096], P(None, 'col', 'grp')
Inputs may be any that keep to these rules, and one draw needn't show every extreme that they name: `tile_row`: slot t belongs to group t // 8; a used slot names one of the group's 4 block rows; empty slots are -1 here and in tile_col at the same places; every group uses two fifths of its 8 slots or more, some group all of them, and a group's used slots lie anywhere among its slots. Two slots may name the same tile position, and their tiles then add. `tile_col`: A used slot names any initial block column of the slab. Initial block row p is stored as storage block row_place[p], in group row_place[p] // 4.
All inputs are finite; a program needn't handle non-finite values.
Results may differ from a plain program's by a relative error of at most 0.005.
Values may be sent and summed in bfloat16 or wider, within the bound.
A program may use at most 128 MiB of HBM per device.

v0:
```python
import jax
import jax.numpy as jnp
from jax import lax
from jax.sharding import PartitionSpec as P

STEPS = 2


def row_sums(product, rows_onehot):
    group_rows = rows_onehot.shape[1]
    totals = [
        jnp.sum(product * rows_onehot[:, row_number][None, :, None], axis=1)
        for row_number in range(group_rows)
    ]
    return jnp.stack(totals, axis=1)


def tile_product(panels, tiles, rows_onehot, source):
    chosen = jnp.take(panels, source, axis=1)
    product = jnp.einsum("osj,sij->osi", chosen, tiles, preferred_element_type=jnp.float32)
    return row_sums(product, rows_onehot)


def tile_pair(panels, first_tiles, second_tiles, rows_onehot, source):
    chosen = jnp.take(panels, source, axis=1)
    first_product = jnp.einsum(
        "osj,sij->osi", chosen, first_tiles, preferred_element_type=jnp.float32
    )
    second_product = jnp.einsum(
        "osj,sij->osi", chosen, second_tiles, preferred_element_type=jnp.float32
    )
    return (row_sums(first_product, rows_onehot), row_sums(second_product, rows_onehot))


def gather_state(current):
    return lax.all_gather(current, "grp", axis=2, tiled=True)


def on_device(orbitals, cosine_tiles, sine_tiles, tile_row, tile_col, row_place):
    halves, orbital_count, rows_dev = orbitals.shape
    tile_size = cosine_tiles.shape[-1]
    group_rows = rows_dev // tile_size
    slab_blocks = row_place.shape[0]
    columns = halves * orbital_count
    blocks = jnp.arange(slab_blocks, dtype=jnp.int32)
    source = jnp.sum(jnp.where(tile_col[:, None] == blocks[None, :], row_place[None, :], 0), axis=1)
    rows_onehot = (tile_row[:, None] == jnp.arange(group_rows, dtype=jnp.int32)[None, :]).astype(
        jnp.float32
    )
    current = orbitals
    cosine_all = cosine_tiles
    sine_all = sine_tiles
    for update in range(STEPS):
        panels = gather_state(current).reshape(columns, slab_blocks, tile_size)
        if update == 0:
            cosine_all, sine_all = (
                lax.all_gather(cosine_tiles, "col", axis=0, tiled=True),
                lax.all_gather(sine_tiles, "col", axis=0, tiled=True),
            )
            direct = tile_product(panels, cosine_all, rows_onehot, source)
        else:
            direct = tile_product(panels, cosine_all, rows_onehot, source)
        spread = direct.astype(jnp.bfloat16).reshape(halves, orbital_count, rows_dev)
        spread_all = lax.all_gather(spread, "grp", axis=2, tiled=True).reshape(
            columns, slab_blocks, tile_size
        )
        cosine_part, sine_part = tile_pair(spread_all, cosine_all, sine_all, rows_onehot, source)
        previous = current.astype(jnp.float32).reshape(columns, group_rows, tile_size)
        real_new = (
            2.0 * (cosine_part[:orbital_count] + sine_part[orbital_count:])
            - previous[:orbital_count]
        )
        imag_new = (
            2.0 * (cosine_part[orbital_count:] - sine_part[:orbital_count])
            - previous[orbital_count:]
        )
        current = (
            jnp.concatenate([real_new, imag_new], axis=0)
            .astype(jnp.bfloat16)
            .reshape(halves, orbital_count, rows_dev)
        )
    return current


def solution(mesh):
    in_specs = (
        P(None, "col", "grp"),
        P(("grp", "col"), None, None),
        P(("grp", "col"), None, None),
        P("grp"),
        P("grp"),
        P(),
    )
    out_specs = P(None, "col", "grp")
    return jax.shard_map(
        on_device, mesh=mesh, in_specs=in_specs, out_specs=out_specs, check_vma=False
    )
```

profile of v0, /device:TPU:0, one launch (start us, length us, event | category | flops | bytes accessed | tf_op | source)
XLA Modules:
  0.0 896.6 jit_solution(8497386573425850756)
XLA Ops:
  6.5 0.7 all-gather.7.cloned.1.call-update
  7.3 0.7 all-gather.9.cloned.1.call-update
  8.3 134.9 %all-gather.7.cloned.1.call-done = bf16[2,832,4096]{2,1,0:T(8,128)(2,1)} async-done(((bf16[2,832,1024]{2,1,0:T(8,128)(2,1)}), bf16[2,832,4096]{2,1,0:T(8,128)(2,1)}) %all-gather.7.cloned.1.call-update) | async-done | bytes 13631504 | tf_op jit(solution)/shard_map/all_gather | solution.py:36
  143.2 8.7 copy.25
  151.9 7.9 copy.19
  159.8 8.7 gather_fusion
  168.5 8.2 multiply_reduce_fusion.23
  176.7 0.5 pad_maximum_fusion.4
  177.2 13.0 %copy.20 = bf16[1664,4,256]{2,1,0:T(4,128)(2,1)S(1)} copy(bf16[1664,4,256]{2,0,1:T(8,128)(2,1)S(1)} %pad_maximum_fusion.4) | data formatting | bytes 6815744 | tf_op jit(solution)/shard_map/stack | solution.py:15
  190.2 3.7 convert_element_type.30
  194.0 0.5 all-gather.13.cloned.1.call-update
  194.6 1.3 copy-done.1
  195.9 3.7 fusion.38
  199.5 4.5 slice.87
  204.1 5.5 slice.91
  209.6 115.7 %all-gather.11.cloned.1.call-done = bf16[2,832,4096]{2,1,0:T(8,128)(2,1)} async-done(((bf16[2,832,1024]{2,1,0:T(8,128)(2,1)}), bf16[2,832,4096]{2,1,0:T(8,128)(2,1)}) %all-gather.11.cloned.1.call-update) | async-done | bytes 13631504 | tf_op jit(solution)/shard_map/all_gather | solution.py:64
  325.3 8.7 copy.26
  334.1 7.9 copy.21
  341.9 8.7 gather_fusion.1
  350.6 10.0 %fusion.8 = f32[8,1664,256]{2,1,0:T(8,128)} fusion(bf16[8,256,256]{2,1,0:T(8,128)(2,1)} %all-gather.9.cloned.1.call-done, bf16[8,1664,256]{2,1,0:T(8,128)(2,1)} %gather_fusion.1, pred[8]{0:T(512)(128)(4,1)S(1)} %compare_and_fusion), kind=kOutput, calls=%fused_computation.40 | convolution fusion | flops 1748238336 | bytes 21495816 | tf_op jit(solution)/shard_map/osj,sij->osi/dot_general | solution.py:26
  360.6 20.3 %multiply_reduce_fusion.15 = (f32[1664,256]{1,0:T(8,128)}, f32[1664,256]{1,0:T(8,128)}, f32[1664,256]{1,0:T(8,128)}, f32[1664,256]{1,0:T(8,128)}, f32[1664,256]{...) fusion(f32[8]{0:T(128)S(1)} %get-tuple-element.49, f32[8]{0:T(128)S(1)} %get-tuple-element.47, ...), kind=kOutput, calls=%fused_computation.19 | convolution fusion | flops 1799356416 | bytes 35127432 | tf_op jit(solution)/shard_map/osj,sij->osi/dot_general | solution.py:29
  380.9 5.2 stack.105
  386.2 4.7 stack.106
  390.9 4.7 stack.107
  395.7 4.7 stack.108
  400.4 4.7 stack.110
  405.2 4.7 stack.111
  409.9 4.7 stack.112
  414.6 4.9 stack.113
  419.6 12.8 %pad_maximum_fusion = (f32[1664,4,256]{2,1,0:T(4,128)S(1)}, f32[1664,4,256]{2,1,0:T(4,128)S(1)}) fusion(f32[1664,1,256]{2,1,0:T(1,128)S(1)} %stack.108, f32[1664,1,256]{2,1,0:T(1,128)S(1)} %stack.107, f32[1664,1,256]{2,1,0:T(1,128)S(1)} %stack.106, f32[1664,1,256]{2,1,0:T(1,128)S(1)} %stack.105, f32[1664,1,256]{2,1,0:T(1,128)S(1)} %stack.113, ...), kind=kLoop, calls=%fused_computation.28 | loop fusion | flops 10223616 | bytes 27262976 | tf_op jit(solution)/shard_map/stack | solution.py:15
  432.4 3.0 fusion.27
  435.4 11.4 %pad_maximum_fusion.5 = bf16[1664,4,256]{2,1,0:T(4,128)(2,1)S(1)} fusion(bf16[832,4,256]{2,1,0:T(4,128)(2,1)S(1)} %get-tuple-element.41, bf16[832,4,256]{2,1,0:T(4,128)(2,1)S(1)} %get-tuple-element.40), kind=kLoop, calls=%fused_computation.67 | loop fusion | flops 1703936 | bytes 6815744 | tf_op jit(solution)/shard_map/concatenate | solution.py:78
  446.8 3.6 convert_element_type.32
  450.5 131.3 %all-gather.15.cloned.1.call-done = bf16[2,832,4096]{2,1,0:T(8,128)(2,1)} async-done(((bf16[2,832,1024]{2,1,0:T(8,128)(2,1)}), bf16[2,832,4096]{2,1,0:T(8,128)(2,1)}) %all-gather.15.cloned.1.call-update) | async-done | bytes 13631504 | tf_op jit(solution)/shard_map/all_gather | solution.py:36
  581.9 9.1 %copy.27 = bf16[208,8,16,256]{3,2,1,0:T(8,128)(2,1)S(1)} copy(bf16[208,8,16,256]{3,1,2,0:T(8,128)(2,1)} %bitcast.81) | data formatting | bytes 27262976
  591.0 7.9 copy.22
  598.8 8.7 gather_fusion.2
  607.5 7.7 multiply_reduce_fusion.11
  615.3 0.5 pad_maximum_fusion.6
  615.7 13.0 %copy.23 = bf16[1664,4,256]{2,1,0:T(4,128)(2,1)S(1)} copy(bf16[1664,4,256]{2,0,1:T(8,128)(2,1)S(1)} %pad_maximum_fusion.6) | data formatting | bytes 6815744 | tf_op jit(solution)/shard_map/stack | solution.py:15
  628.8 3.7 convert_element_type.33
  632.5 1.9 copy-done
  634.4 3.7 fusion.37
  638.1 4.0 slice.95
  642.2 5.4 slice.99
  647.6 116.3 %all-gather.17.cloned.1.call-done = bf16[2,832,4096]{2,1,0:T(8,128)(2,1)} async-done(((bf16[2,832,1024]{2,1,0:T(8,128)(2,1)}), bf16[2,832,4096]{2,1,0:T(8,128)(2,1)}) %all-gather.17.cloned.1.call-update) | async-done | bytes 13631504 | tf_op jit(solution)/shard_map/all_gather | solution.py:64
  763.9 8.7 copy.28
  772.6 8.0 copy.24
  780.6 8.6 gather_fusion.3
  789.2 10.0 %fusion.2 = f32[8,1664,256]{2,1,0:T(8,128)} fusion(bf16[8,256,256]{2,1,0:T(8,128)(2,1)} %all-gather.9.cloned.1.call-done, bf16[8,1664,256]{2,1,0:T(8,128)(2,1)} %gather_fusion.3, pred[8]{0:T(512)(128)(4,1)S(1)} %compare_and_fusion), kind=kOutput, calls=%fused_computation.34 | convolution fusion | flops 1748238336 | bytes 21495816 | tf_op jit(solution)/shard_map/osj,sij->osi/dot_general | solution.py:26
  799.3 20.3 %multiply_reduce_fusion.3 = (f32[1664,256]{1,0:T(8,128)}, f32[1664,256]{1,0:T(8,128)}, f32[1664,256]{1,0:T(8,128)}, f32[1664,256]{1,0:T(8,128)}, f32[1664,256]{1...) fusion(f32[8]{0:T(128)S(1)} %get-tuple-element.49, f32[8]{0:T(128)S(1)} %get-tuple-element.47, ...), kind=kOutput, calls=%fused_computation.7 | convolution fusion | flops 1799356416 | bytes 35127432 | tf_op jit(solution)/shard_map/osj,sij->osi/dot_general | solution.py:29
  819.6 5.1 stack.120
  824.7 4.7 stack.121
  829.4 4.9 stack.122
  834.4 4.7 stack.123
  839.1 4.7 stack.125
  843.8 4.7 stack.126
  848.6 4.7 stack.127
  853.3 4.7 stack.128
  858.0 6.8 pad_maximum_fusion.2
  864.8 6.5 pad_maximum_fusion.3
  871.3 3.0 fusion.21
  874.3 11.4 %pad_maximum_fusion.7 = bf16[1664,4,256]{2,1,0:T(4,128)(2,1)S(1)} fusion(bf16[832,4,256]{2,1,0:T(4,128)(2,1)S(1)} %get-tuple-element.39, bf16[832,4,256]{2,1,0:T(4,128)(2,1)S(1)} %get-tuple-element.38), kind=kLoop, calls=%fused_computation.69 | loop fusion | flops 1703936 | bytes 6815744 | tf_op jit(solution)/shard_map/concatenate | solution.py:78
  885.7 3.6 convert_element_type.35
  (59 shorter events, 0.6 us)
Async XLA Ops:
  6.5 1.5 copy-start.21
  6.5 1.5 copy-start.20
  6.5 1.8 copy-start.19
  6.5 136.6 %all-gather.7.cloned.1.call-start = ((), (), s32[]{:S(2)}) async-start(), calls=%async_computation | async-start | bytes 17039360 | tf_op jit(solution)/shard_map/all_gather | solution.py:36
  7.3 161.2 %all-gather.9.cloned.1.call-start = ((), (), s32[]{:S(2)}) async-start(), calls=%async_computation.1 | async-start | bytes 1179648 | tf_op jit(solution)/shard_map/all_gather | solution.py:57
  8.0 317.3 %all-gather.11.cloned.1.call-start = ((), (), s32[]{:S(2)}) async-start(), calls=%async_computation.2 | async-start | bytes 17039360 | tf_op jit(solution)/shard_map/all_gather | solution.py:64
  193.9 2.0 copy-start.1
  193.9 166.7 %all-gather.13.cloned.1.call-start = ((), (), s32[]{:S(2)}) async-start(), calls=%async_computation.3 | async-start | bytes 1179648 | tf_op jit(solution)/shard_map/all_gather | solution.py:58
  194.5 387.3 %all-gather.15.cloned.1.call-start = ((), (), s32[]{:S(2)}) async-start(), calls=%async_computation.4 | async-start | bytes 17039360 | tf_op jit(solution)/shard_map/all_gather | solution.py:36
  380.9 5.2 copy-start.18
  380.9 10.0 %copy-start.17 = (f32[1664,256]{1,0:T(8,128)S(1)}, f32[1664,256]{1,0:T(8,128)}, u32[]{:S(2)}) copy-start(f32[1664,256]{1,0:T(8,128)} %get-tuple-element.31) | copy-start | bytes 5111812
  386.2 9.5 %copy-start.16 = (f32[1664,256]{1,0:T(8,128)S(1)}, f32[1664,256]{1,0:T(8,128)}, u32[]{:S(2)}) copy-start(f32[1664,256]{1,0:T(8,128)} %get-tuple-element.32) | copy-start | bytes 5111812
  390.9 9.5 %copy-start.15 = (f32[1664,256]{1,0:T(8,128)S(1)}, f32[1664,256]{1,0:T(8,128)}, u32[]{:S(2)}) copy-start(f32[1664,256]{1,0:T(8,128)} %get-tuple-element.22) | copy-start | bytes 5111812
  395.7 9.5 %copy-start.14 = (f32[1664,256]{1,0:T(8,128)S(1)}, f32[1664,256]{1,0:T(8,128)}, u32[]{:S(2)}) copy-start(f32[1664,256]{1,0:T(8,128)} %get-tuple-element.25) | copy-start | bytes 5111812
  400.4 9.5 %copy-start.13 = (f32[1664,256]{1,0:T(8,128)S(1)}, f32[1664,256]{1,0:T(8,128)}, u32[]{:S(2)}) copy-start(f32[1664,256]{1,0:T(8,128)} %get-tuple-element.24) | copy-start | bytes 5111812
  405.1 9.5 %copy-start.11 = (f32[1664,256]{1,0:T(8,128)S(1)}, f32[1664,256]{1,0:T(8,128)}, u32[]{:S(2)}) copy-start(f32[1664,256]{1,0:T(8,128)} %get-tuple-element.23) | copy-start | bytes 5111812
  419.5 12.8 %copy-start.3 = (f32[832,4,256]{2,1,0:T(4,128)S(1)}, f32[832,4,256]{2,1,0:T(4,128)}, u32[]{:S(2)}) copy-start(f32[832,4,256]{2,1,0:T(4,128)} %slice.91) | copy-start | bytes 10223620
  450.5 313.4 %all-gather.17.cloned.1.call-start = ((), (), s32[]{:S(2)}) async-start(), calls=%async_computation.5 | async-start | bytes 17039360 | tf_op jit(solution)/shard_map/all_gather | solution.py:64
  598.8 8.7 copy-start.4
  632.5 2.0 copy-start
  819.6 5.1 copy-start.12
  819.6 9.8 %copy-start.10 = (f32[1664,256]{1,0:T(8,128)S(1)}, f32[1664,256]{1,0:T(8,128)}, u32[]{:S(2)}) copy-start(f32[1664,256]{1,0:T(8,128)} %get-tuple-element.35) | copy-start | bytes 5111812
  824.6 9.7 %copy-start.9 = (f32[1664,256]{1,0:T(8,128)S(1)}, f32[1664,256]{1,0:T(8,128)}, u32[]{:S(2)}) copy-start(f32[1664,256]{1,0:T(8,128)} %get-tuple-element.36) | copy-start | bytes 5111812
  829.4 9.7 %copy-start.8 = (f32[1664,256]{1,0:T(8,128)S(1)}, f32[1664,256]{1,0:T(8,128)}, u32[]{:S(2)}) copy-start(f32[1664,256]{1,0:T(8,128)} %get-tuple-element.10) | copy-start | bytes 5111812
  834.3 9.5 %copy-start.7 = (f32[1664,256]{1,0:T(8,128)S(1)}, f32[1664,256]{1,0:T(8,128)}, u32[]{:S(2)}) copy-start(f32[1664,256]{1,0:T(8,128)} %get-tuple-element.13) | copy-start | bytes 5111812
  839.1 9.5 %copy-start.6 = (f32[1664,256]{1,0:T(8,128)S(1)}, f32[1664,256]{1,0:T(8,128)}, u32[]{:S(2)}) copy-start(f32[1664,256]{1,0:T(8,128)} %get-tuple-element.12) | copy-start | bytes 5111812
  843.8 9.5 %copy-start.5 = (f32[1664,256]{1,0:T(8,128)S(1)}, f32[1664,256]{1,0:T(8,128)}, u32[]{:S(2)}) copy-start(f32[1664,256]{1,0:T(8,128)} %get-tuple-element.11) | copy-start | bytes 5111812
  864.8 6.5 copy-start.2
Sparse Core Ops, SparseCore 0:
  9.2 133.9 all-gather.6
  144.8 22.0 all-gather.8
  194.0 131.2 all-gather.10
  326.8 22.0 all-gather.12
  450.6 131.2 all-gather.14
  632.6 131.2 all-gather.16
where the time goes:
time: 903 us; the launch traced here: 897 us
  waiting for transfers between devices  500 us (55%)
  local copies, waits for them, and re-layouts  249 us (28%)
  matrix products  76.6 us (8%)
  other arithmetic  56 us (6%)
  between operations  14.5 us (2%)
    all_gather x2, waiting for transfers between devices, gather_state(): return lax.all_gather(current, 'grp', axis=2, tiled=True)  266 us
    all_gather x2, waiting for transfers between devices, on_device(): lax.all_gather(spread, 'grp', axis=2, tiled=True)  232 us
    another operation x18, local copies, waits for them, and re-layouts, row_sums(): return jnp.stack(totals, axis=1)  103 us
    dot_general x2, matrix products, tile_pair(): jnp.einsum('osj,sij->osi', chosen, second_tiles, preferred_element_type=j...  40.6 us
    unnamed x48, local copies, waits for them, and re-layouts  38.6 us
    another operation x5, other arithmetic, row_sums(): return jnp.stack(totals, axis=1)  27 us
    concatenate x2, other arithmetic, on_device(): jnp.concatenate([real_new, imag_new], axis=0).astype(jnp.bfloat16)  22.8 us
    dot_general x2, matrix products, tile_pair(): jnp.einsum('osj,sij->osi', chosen, first_tiles, preferred_element_type=jn...  20.1 us
  transfers between devices with their start and end apart: 6, of which 4 were waited for; matrix products, arithmetic and copies ran while one was open for 10% of the time, Pallas kernels for 0%

commit v1 on v0

v1 whole, which is shorter than its diff:
```python
import functools

import jax
import jax.numpy as jnp
from jax import lax
from jax.experimental import pallas as pl
from jax.experimental.pallas import tpu as pltpu
from jax.sharding import PartitionSpec as P

STEPS = 2
ROW_TILE = 16
CHUNKS = 2
MESH = pl.DeviceIdType.MESH
VMEM_LIMIT = 48 * 2**20


def row_sums(product, rows_onehot):
    group_rows = rows_onehot.shape[1]
    totals = [
        jnp.sum(product * rows_onehot[:, row_number][None, :, None], axis=1)
        for row_number in range(group_rows)
    ]
    return jnp.stack(totals, axis=1)


def tile_product(panels, tiles, rows_onehot, source):
    chosen = jnp.take(panels, source, axis=1)
    product = jnp.einsum("osj,sij->osi", chosen, tiles, preferred_element_type=jnp.float32)
    return row_sums(product, rows_onehot)


def find_source(tile_col, row_place):
    blocks = jnp.arange(row_place.shape[0], dtype=jnp.int32)
    return jnp.sum(jnp.where(tile_col[:, None] == blocks[None, :], row_place[None, :], 0), axis=1)


def gather_plan(orbitals, cosine_tiles, sine_tiles, tile_row, tile_col, row_place):
    halves, orbital_count, rows_dev = orbitals.shape
    tile_size = cosine_tiles.shape[-1]
    group_rows = rows_dev // tile_size
    slab_blocks = row_place.shape[0]
    columns = halves * orbital_count
    source = find_source(tile_col, row_place)
    rows_onehot = (tile_row[:, None] == jnp.arange(group_rows, dtype=jnp.int32)[None, :]).astype(
        jnp.float32
    )
    current = orbitals
    cosine_all = lax.all_gather(cosine_tiles, "col", axis=0, tiled=True)
    sine_all = lax.all_gather(sine_tiles, "col", axis=0, tiled=True)
    for _ in range(STEPS):
        panels = lax.all_gather(current, "grp", axis=2, tiled=True).reshape(
            columns, slab_blocks, tile_size
        )
        direct = tile_product(panels, cosine_all, rows_onehot, source)
        spread = direct.astype(jnp.bfloat16).reshape(halves, orbital_count, rows_dev)
        spread_all = lax.all_gather(spread, "grp", axis=2, tiled=True).reshape(
            columns, slab_blocks, tile_size
        )
        cosine_part = tile_product(spread_all, cosine_all, rows_onehot, source)
        sine_part = tile_product(spread_all, sine_all, rows_onehot, source)
        previous = current.astype(jnp.float32).reshape(columns, group_rows, tile_size)
        real_new = (
            2.0 * (cosine_part[:orbital_count] + sine_part[orbital_count:])
            - previous[:orbital_count]
        )
        imag_new = (
            2.0 * (cosine_part[orbital_count:] - sine_part[:orbital_count])
            - previous[orbital_count:]
        )
        current = (
            jnp.concatenate([real_new, imag_new], axis=0)
            .astype(jnp.bfloat16)
            .reshape(halves, orbital_count, rows_dev)
        )
    return current


def slot_lists(tile_row, tile_col, row_place, group_rows):
    slots = tile_row.shape[0]
    number = jnp.arange(slots, dtype=jnp.int32)
    row = jnp.where(tile_row < 0, group_rows, tile_row)
    key = row * slots + number
    rank = jnp.sum((key[None, :] < key[:, None]).astype(jnp.int32), axis=1)
    place = (rank[None, :] == number[:, None]).astype(jnp.int32)
    source = find_source(tile_col, row_place)
    order = jnp.sum(place * number[None, :], axis=1)
    sorted_source = jnp.sum(place * source[None, :], axis=1)
    sorted_row = jnp.sum(place * row[None, :], axis=1)
    before = jnp.concatenate([jnp.full((1,), -1, jnp.int32), sorted_row[:-1]])
    keep = (sorted_row == before).astype(jnp.int32)
    rows = jnp.arange(group_rows, dtype=jnp.int32)
    last = jnp.maximum(jnp.sum((row[None, :] <= rows[:, None]).astype(jnp.int32), axis=1) - 1, 0)
    used = jnp.max((row[None, :] == rows[:, None]).astype(jnp.int32), axis=1)
    table = [order, sorted_source, keep, last, used]
    table = [jnp.pad(line, (0, 128 - line.shape[0])) for line in table]
    return jnp.pad(jnp.stack(table), ((0, 8 - len(table)), (0, 0)))


def dot_t(panel, tile):
    return lax.dot_general(
        panel, tile, (((1,), (1,)), ((), ())), preferred_element_type=jnp.float32
    )


def propagate(current, spread, sums, cosine, sine, table, n_grp, group_rows, slots):
    halves, length, tile_size = current.shape[1:]
    height = halves * length

    def slot_values(g, k):
        return table[g, 0, k], table[g, 1, k], table[g, 2, k].astype(jnp.float32)

    def spread_group(g, carry):
        total = None
        for k in range(slots):
            slot, source, keep = slot_values(g, k)
            panel = current[source].reshape(height, tile_size)
            product = dot_t(panel, cosine[g, slot])
            total = product if k == 0 else product + total * keep
            sums[k, :height] = total
        for r in range(group_rows):
            used = table[g, 4, r].astype(jnp.float32)
            spread[g * group_rows + r, :height] = (sums[table[g, 3, r], :height] * used).astype(
                spread.dtype
            )
        return carry

    def double_group(g, carry):
        total = None
        for k in range(slots):
            slot, source, keep = slot_values(g, k)
            panel = spread[source, :height]
            by_cosine = dot_t(panel, cosine[g, slot])
            by_sine = dot_t(panel, sine[g, slot])
            product = jnp.concatenate(
                [by_cosine[:length] + by_sine[length:], by_cosine[length:] - by_sine[:length]],
                axis=0,
            )
            total = product if k == 0 else product + total * keep
            sums[k, :height] = total
        for r in range(group_rows):
            used = table[g, 4, r].astype(jnp.float32)
            block = g * group_rows + r
            previous = current[block].reshape(height, tile_size).astype(jnp.float32)
            new = 2.0 * (sums[table[g, 3, r], :height] * used) - previous
            current[block] = new.astype(current.dtype).reshape(halves, length, tile_size)
        return carry

    def step(_, carry):
        lax.fori_loop(0, n_grp, spread_group, 0)
        lax.fori_loop(0, n_grp, double_group, 0)
        return carry

    lax.fori_loop(0, STEPS, step, 0)


def kernel(n_grp, n_z, cuts, group_rows, orb, cos_in, sin_in, lists, out, *scratch):
    currents = scratch[: len(cuts)]
    (
        spread,
        sums,
        cosine,
        sine,
        table_v,
        table,
        list_send,
        list_recv,
        table_sem,
        lane_send,
        lane_recv,
        pair_send,
        pair_recv,
        own_sem,
        in_send,
        in_recv,
        in_local,
        out_send,
        out_recv,
        out_local,
    ) = scratch[len(cuts) :]
    tile_size = cosine.shape[-1]
    slots = cosine.shape[1]
    share = orb.shape[1] // n_grp
    grp, col = lax.axis_index("grp"), lax.axis_index("col")
    z, core = col // 2, col % 2
    tiles = (cosine, sine)
    own = (cos_in.at[0], sin_in.at[0])

    def grp_at(shift):
        return lax.rem(grp + shift + n_grp, n_grp)

    def z_at(shift):
        return lax.rem(z + shift + n_z, n_z)

    def device(dg, dz):
        return (grp_at(dg), z_at(dz) * 2 + core)

    pair = (grp, z * 2 + 1 - core)
    sent = []

    def remote(src, dst, send_sem, recv_sem, to):
        return pltpu.make_async_remote_copy(
            src_ref=src,
            dst_ref=dst,
            send_sem=send_sem,
            recv_sem=recv_sem,
            device_id=to,
            device_id_type=MESH,
        )

    def start(copy):
        copy.start()
        sent.append(copy)

    barrier = pltpu.get_barrier_semaphore()
    partners = [device(s, 0) for s in range(1, n_grp)]
    partners += [device(0, s) for s in range(1, n_z)] + [pair]
    for partner in partners:
        pl.semaphore_signal(barrier, inc=1, device_id=partner, device_id_type=MESH)
    pl.semaphore_wait(barrier, len(partners))

    def tile_ref(k, tg, tz, lane):
        return tiles[k].at[grp_at(-tg), z_at(-tz) * 2 + lane]

    def lane_copy(k, tg, tz, dg, dz):
        dst = tile_ref(k, tg, tz, core)
        src = own[k] if (tg, tz) == (0, 0) else dst
        at = (k, tg + dg, tz + dz)
        start(remote(src, dst, lane_send.at[at], lane_recv.at[at], device(dg, dz)))

    def lane_wait(k, sg, sz):
        ref = tile_ref(k, sg, sz, core)
        at = (k, sg, sz)
        remote(ref, ref, lane_send.at[at], lane_recv.at[at], pair).wait_recv()

    def pair_copy(k, sg, sz):
        dst = tile_ref(k, sg, sz, core)
        src = own[k] if (sg, sz) == (0, 0) else dst
        at = (k, sg, sz)
        start(remote(src, dst, pair_send.at[at], pair_recv.at[at], pair))

    def pair_wait(k, sg, sz):
        ref = tile_ref(k, sg, sz, 1 - core)
        at = (k, sg, sz)
        remote(ref, ref, pair_send.at[at], pair_recv.at[at], pair).wait_recv()

    for s in range(1, n_grp):
        start(remote(lists, table_v.at[grp], list_send.at[s], list_recv.at[s], device(s, 0)))
    for s in range(1, n_z):
        lane_copy(0, 0, 0, 0, s)
    for s in range(1, n_grp):
        lane_copy(1, 0, 0, s, 0)
    local = [pltpu.make_async_copy(lists, table_v.at[grp], own_sem.at[2])]
    for k in range(2):
        local.append(pltpu.make_async_copy(own[k], tile_ref(k, 0, 0, core), own_sem.at[k]))
    for copy in local:
        copy.start()
    for k in range(2):
        pair_copy(k, 0, 0)
    for s in range(1, n_grp):
        lane_copy(0, 0, 0, s, 0)
    for s in range(1, n_z):
        lane_copy(1, 0, 0, 0, s)

    def in_piece(c, s, r):
        begin, length = cuts[c]
        rows = pl.ds(pl.multiple_of(grp_at(s) * share + begin, ROW_TILE), length)
        src = orb.at[:, rows, pl.ds(r * tile_size, tile_size)]
        return src, currents[c].at[grp * group_rows + r]

    for c in range(len(cuts)):
        for r in range(group_rows):
            src, dst = in_piece(c, 0, r)
            pltpu.make_async_copy(src, dst, in_local.at[c, r]).start()
            for s in range(1, n_grp):
                src, dst = in_piece(c, s, r)
                at = (c, s, r)
                start(remote(src, dst, in_send.at[at], in_recv.at[at], device(s, 0)))

    for s in range(1, max(n_grp, n_z)):
        if s < n_z:
            lane_wait(0, 0, s)
            for d in range(1, n_grp):
                lane_copy(0, 0, s, d, 0)
            pair_copy(0, 0, s)
        if s < n_grp:
            lane_wait(1, s, 0)
            for d in range(1, n_z):
                lane_copy(1, s, 0, 0, d)
            pair_copy(1, s, 0)
    for sz in range(n_z):
        for sg in range(1, n_grp):
            lane_wait(0, sg, sz)
            pair_copy(0, sg, sz)
    for sg in range(n_grp):
        for sz in range(1, n_z):
            lane_wait(1, sg, sz) if sg or sz else None
            pair_copy(1, sg, sz)
    for copy in local:
        copy.wait()
    for s in range(1, n_grp):
        ref = table_v.at[grp_at(-s)]
        remote(ref, ref, list_send.at[s], list_recv.at[s], pair).wait_recv()
    to_scalar = pltpu.make_async_copy(table_v, table, table_sem.at[0])
    to_scalar.start()
    to_scalar.wait()
    for k in range(2):
        for sg in range(n_grp):
            for sz in range(n_z):
                pair_wait(k, sg, sz)

    def out_piece(c, s, r):
        begin, length = cuts[c]
        rows = pl.ds(pl.multiple_of(grp * share + begin, ROW_TILE), length)
        dst = out.at[:, rows, pl.ds(r * tile_size, tile_size)]
        return currents[c].at[grp_at(s) * group_rows + r], dst

    def landing(c, s, r):
        begin, length = cuts[c]
        rows = pl.ds(pl.multiple_of(grp_at(-s) * share + begin, ROW_TILE), length)
        return out.at[:, rows, pl.ds(r * tile_size, tile_size)]

    for c in range(len(cuts)):
        for r in range(group_rows):
            src, dst = in_piece(c, 0, r)
            pltpu.make_async_copy(src, dst, in_local.at[c, r]).wait()
            for s in range(1, n_grp):
                ref = currents[c].at[grp_at(-s) * group_rows + r]
                at = (c, s, r)
                remote(ref, ref, in_send.at[at], in_recv.at[at], pair).wait_recv()
        propagate(
            currents[c], spread, sums, cosine, sine, table, n_grp, group_rows, slots
        )
        for r in range(group_rows):
            for s in range(1, n_grp):
                src, dst = out_piece(c, s, r)
                at = (c, s, r)
                start(remote(src, dst, out_send.at[at], out_recv.at[at], device(s, 0)))
            src, dst = out_piece(c, 0, r)
            pltpu.make_async_copy(src, dst, out_local.at[c, r]).start()
    for c in range(len(cuts)):
        for r in range(group_rows):
            src, dst = out_piece(c, 0, r)
            pltpu.make_async_copy(src, dst, out_local.at[c, r]).wait()
            for s in range(1, n_grp):
                ref = landing(c, s, r)
                at = (c, s, r)
                remote(ref, ref, out_send.at[at], out_recv.at[at], pair).wait_recv()
    for copy in sent:
        copy.wait_send()


def chunk_cuts(share):
    pieces = share // ROW_TILE
    count = min(CHUNKS, pieces)
    sizes = [(pieces // count + (c < pieces % count)) * ROW_TILE for c in range(count)]
    return [(sum(sizes[:c]), sizes[c]) for c in range(count)]


def exchange_plan(n_grp, n_col, orbitals, cosine_tiles, sine_tiles, tile_row, tile_col, row_place):
    halves, orbital_count, rows_dev = orbitals.shape
    tile_size = cosine_tiles.shape[-1]
    group_rows = rows_dev // tile_size
    slots = tile_row.shape[0]
    blocks = row_place.shape[0]
    n_z = n_col // 2
    cuts = chunk_cuts(orbital_count // n_grp)
    tallest = halves * max(length for _, length in cuts)
    lists = slot_lists(tile_row, tile_col, row_place, group_rows)
    dma = pltpu.SemaphoreType.DMA
    grid = (len(cuts), n_grp, group_rows)
    scratch = [
        pltpu.VMEM((blocks, halves, length, tile_size), orbitals.dtype) for _, length in cuts
    ]
    scratch += [
        pltpu.VMEM((blocks, tallest, tile_size), jnp.bfloat16),
        pltpu.VMEM((slots, tallest, tile_size), jnp.float32),
        pltpu.VMEM((n_grp, slots, tile_size, tile_size), cosine_tiles.dtype),
        pltpu.VMEM((n_grp, slots, tile_size, tile_size), sine_tiles.dtype),
        pltpu.VMEM((n_grp,) + lists.shape, jnp.int32),
        pltpu.SMEM((n_grp,) + lists.shape, jnp.int32),
        dma((n_grp,)),
        dma((n_grp,)),
        dma((1,)),
        dma((2, n_grp, n_z)),
        dma((2, n_grp, n_z)),
        dma((2, n_grp, n_z)),
        dma((2, n_grp, n_z)),
        dma((3,)),
        dma(grid),
        dma(grid),
        dma((len(cuts), group_rows)),
        dma(grid),
        dma(grid),
        dma((len(cuts), group_rows)),
    ]
    return pl.pallas_call(
        functools.partial(kernel, n_grp, n_z, cuts, group_rows),
        out_shape=jax.ShapeDtypeStruct(orbitals.shape, orbitals.dtype),
        in_specs=[pl.BlockSpec(memory_space=pl.ANY)] * 4,
        out_specs=pl.BlockSpec(memory_space=pl.ANY),
        scratch_shapes=scratch,
        compiler_params=pltpu.CompilerParams(
            collective_id=0, has_side_effects=True, vmem_limit_bytes=VMEM_LIMIT
        ),
    )(orbitals, cosine_tiles, sine_tiles, lists)


def on_device(n_grp, n_col, orbitals, cosine_tiles, *rest):
    halves, orbital_count, rows_dev = orbitals.shape
    tile_size = cosine_tiles.shape[-1]
    slots = rest[1].shape[0]
    tile_bytes = 2 * n_grp * slots * tile_size * tile_size * 2
    fits = tile_bytes + 4 * orbitals.size * 2 < VMEM_LIMIT
    even = orbital_count % (n_grp * ROW_TILE) == 0 and tile_size % 128 == 0
    paired = n_col % 2 == 0 and slots == n_col and slots <= 128
    if fits and even and paired and n_grp > 1 and n_col > 2:
        return exchange_plan(n_grp, n_col, orbitals, cosine_tiles, *rest)
    return gather_plan(orbitals, cosine_tiles, *rest)


def solution(mesh):
    in_specs = (
        P(None, "col", "grp"),
        P(("grp", "col"), None, None),
        P(("grp", "col"), None, None),
        P("grp"),
        P("grp"),
        P(),
    )
    out_specs = P(None, "col", "grp")
    return jax.shard_map(
        functools.partial(on_device, mesh.shape["grp"], mesh.shape["col"]),
        mesh=mesh,
        in_specs=in_specs,
        out_specs=out_specs,
        check_vma=False,
    )
```

time: 903 us -> 134 us (0.15)
  waiting for transfers between devices: 500 us -> 0 us
  local copies, waits for them, and re-layouts: 249 us -> 3.6 us
  Pallas kernels: 0 us -> 128 us
  matrix products: 76.6 us -> 0 us
  other arithmetic: 56 us -> 2.09 us
  between operations: 14.5 us -> 0.04 us
    all_gather x6 -> x0, waiting for transfers between devices: 498 us -> none  [the longest x2 266 us: gather_state(): return lax.all_gather(current, 'grp', axis=2, tiled=True)]
    pallas_call x0 -> x1, Pallas kernels: none -> 128 us  [exchange_plan(): pl.pallas_call(functools.partial(kernel, n_grp, n_z, cuts, group_rows), o...]
    another operation x18 -> x3, local copies, waits for them, and re-layouts: 103 us -> 0.04 us  [slot_lists(): return jnp.pad(jnp.stack(table), ((0, 8 - len(table)), (0, 0)))]
    dot_general x6 -> x0, matrix products: 76.6 us -> none  [the longest x2 40.6 us: tile_pair(): jnp.einsum('osj,sij->osi', chosen, second_tiles, preferred_element_type=j...]
    unnamed x48 -> x5, local copies, waits for them, and re-layouts: 38.6 us -> 3.56 us
    gather x4 -> x0, local copies, waits for them, and re-layouts: 34.6 us -> none  [the longest x2 17.4 us: tile_product(): chosen = jnp.take(panels, source, axis=1)]
    another operation x7 -> x1, other arithmetic: 33 us -> 0.01 us  [slot_lists(): return jnp.pad(jnp.stack(table), ((0, 8 - len(table)), (0, 0)))]
    reshape x4 -> x0, local copies, waits for them, and re-layouts: 31.6 us -> none  [the longest x2 15.9 us: on_device(): lax.all_gather(spread, 'grp', axis=2, tiled=True)]
  transfers between devices with their start and end apart: 6 -> 0, of which waited for: 4 -> 0; matrix products, arithmetic and copies ran while one was open for 10% -> 0% of each run, Pallas kernels for 0% -> 0%
where the time goes in v1:
time: 134 us
  Pallas kernels  128 us (96%)
  local copies, waits for them, and re-layouts  3.6 us (3%)
  other arithmetic  2.09 us (2%)
    pallas_call x1, Pallas kernels, exchange_plan(): pl.pallas_call(functools.partial(kernel, n_grp, n_z, cuts, group_rows), o...  128 us
    unnamed x5, local copies, waits for them, and re-layouts  3.56 us

profile of v1, /device:TPU:0, one launch (start us, length us, event | category | flops | bytes accessed | tf_op | source)
XLA Modules:
  0.0 133.7 jit_solution(11703092104887158830)
XLA Ops:
  0.0 0.9 select_reduce_fusion.2
  0.9 0.7 iota_add_fusion
  1.5 0.2 convert_reduce_fusion
  1.7 0.1 select_reduce_fusion
  1.9 0.1 add_compare_fusion
  1.9 0.2 convert_reduce_fusion.1
  2.2 0.0 copy-start
  2.2 0.9 copy-done
  3.1 0.0 copy-start.1
  3.1 0.9 copy-done.1
  4.0 127.9 %shard_map.64 = bf16[2,832,1024]{2,1,0:T(8,128)(2,1)S(1)} custom-call(bf16[2,832,1024]{2,1,0:T(8,128)(2,1)} %orb.1, bf16[1,256,256]{2,1,0:T(8,128)(2,1)S(1)} %copy-done, bf16[1,256,256]{2,1,0:T(8,128)(2,1)S(1)} %copy-done.1, s32[8,128]{1,0:T(8,128)S(1)} %pad.27.lists), custom_call_target="tpu_custom_call" | custom-call | tf_op jit(solution)/shard_map/pallas_call | solution.py:396
  131.9 1.8 %copy.8 = bf16[2,832,1024]{2,1,0:T(8,128)(2,1)} copy(bf16[2,832,1024]{2,1,0:T(8,128)(2,1)S(1)} %shard_map.64) | data formatting | bytes 6815744
  (6 shorter events, 0.1 us)
Async XLA Ops:
  2.2 0.9 copy-start
  3.1 0.9 copy-start.1

commit v2 on v1

--- a/solution.py
+++ b/solution.py
@@ -9,7 +9,7 @@
 
 STEPS = 2
 ROW_TILE = 16
-CHUNKS = 2
+CHUNKS = 3
 MESH = pl.DeviceIdType.MESH
 VMEM_LIMIT = 48 * 2**20
 
@@ -102,7 +102,7 @@
     )
 
 
-def propagate(current, spread, sums, cosine, sine, table, n_grp, group_rows, slots):
+def stages(current, spread, sums, cosine, sine, table, group_rows, slots):
     halves, length, tile_size = current.shape[1:]
     height = halves * length
 
@@ -145,12 +145,7 @@
             current[block] = new.astype(current.dtype).reshape(halves, length, tile_size)
         return carry
 
-    def step(_, carry):
-        lax.fori_loop(0, n_grp, spread_group, 0)
-        lax.fori_loop(0, n_grp, double_group, 0)
-        return carry
-
-    lax.fori_loop(0, STEPS, step, 0)
+    return spread_group, double_group
 
 
 def kernel(n_grp, n_z, cuts, group_rows, orb, cos_in, sin_in, lists, out, *scratch):
@@ -185,8 +180,8 @@
     tiles = (cosine, sine)
     own = (cos_in.at[0], sin_in.at[0])
 
-    def grp_at(shift):
-        return lax.rem(grp + shift + n_grp, n_grp)
+    def grp_at(diff):
+        return lax.rem(grp // 2 + diff // 2, 2) * 2 + lax.rem(grp + diff, 2)
 
     def z_at(shift):
         return lax.rem(z + shift + n_z, n_z)
@@ -219,13 +214,13 @@
     pl.semaphore_wait(barrier, len(partners))
 
     def tile_ref(k, tg, tz, lane):
-        return tiles[k].at[grp_at(-tg), z_at(-tz) * 2 + lane]
+        return tiles[k].at[grp_at(tg), z_at(-tz) * 2 + lane]
 
     def lane_copy(k, tg, tz, dg, dz):
         dst = tile_ref(k, tg, tz, core)
         src = own[k] if (tg, tz) == (0, 0) else dst
-        at = (k, tg + dg, tz + dz)
-        start(remote(src, dst, lane_send.at[at], lane_recv.at[at], device(dg, dz)))
+        at = (k, tg ^ dg, (tz + dz) % n_z)
+        return remote(src, dst, lane_send.at[at], lane_recv.at[at], device(dg, dz))
 
     def lane_wait(k, sg, sz):
         ref = tile_ref(k, sg, sz, core)
@@ -243,12 +238,28 @@
         at = (k, sg, sz)
         remote(ref, ref, pair_send.at[at], pair_recv.at[at], pair).wait_recv()
 
-    for s in range(1, n_grp):
+    guarded = []
+
+    def start_if(condition, copy):
+        guarded.append((condition, copy))
+        pl.when(condition)(copy.start)
+
+    def pass_on(sg, sz):
+        below = z >= sz
+        up, down = z < n_z - 1, z > 0
+        if sz:
+            up, down = jnp.logical_and(up, below), jnp.logical_and(down, jnp.logical_not(below))
+        start_if(up, lane_copy(1, sg, sz, 0, 1))
+        start_if(down, lane_copy(1, sg, sz, 0, -1))
+
+    others = range(1, n_grp)
+    for s in others:
         start(remote(lists, table_v.at[grp], list_send.at[s], list_recv.at[s], device(s, 0)))
+    for s in others:
+        start(lane_copy(1, 0, 0, s, 0))
     for s in range(1, n_z):
-        lane_copy(0, 0, 0, 0, s)
-    for s in range(1, n_grp):
-        lane_copy(1, 0, 0, s, 0)
+        start(lane_copy(0, 0, 0, 0, s))
+    pass_on(0, 0)
     local = [pltpu.make_async_copy(lists, table_v.at[grp], own_sem.at[2])]
     for k in range(2):
         local.append(pltpu.make_async_copy(own[k], tile_ref(k, 0, 0, core), own_sem.at[k]))
@@ -256,10 +267,8 @@
         copy.start()
     for k in range(2):
         pair_copy(k, 0, 0)
-    for s in range(1, n_grp):
-        lane_copy(0, 0, 0, s, 0)
-    for s in range(1, n_z):
-        lane_copy(1, 0, 0, 0, s)
+    for s in (1, 2):
+        start(lane_copy(0, 0, 0, s, 0))
 
     def in_piece(c, s, r):
         begin, length = cuts[c]
@@ -267,43 +276,55 @@
         src = orb.at[:, rows, pl.ds(r * tile_size, tile_size)]
         return src, currents[c].at[grp * group_rows + r]
 
-    for c in range(len(cuts)):
+    def send_orbitals(c):
         for r in range(group_rows):
             src, dst = in_piece(c, 0, r)
             pltpu.make_async_copy(src, dst, in_local.at[c, r]).start()
-            for s in range(1, n_grp):
+            for s in (3, 1, 2):
                 src, dst = in_piece(c, s, r)
                 at = (c, s, r)
                 start(remote(src, dst, in_send.at[at], in_recv.at[at], device(s, 0)))
 
-    for s in range(1, max(n_grp, n_z)):
-        if s < n_z:
-            lane_wait(0, 0, s)
-            for d in range(1, n_grp):
-                lane_copy(0, 0, s, d, 0)
-            pair_copy(0, 0, s)
-        if s < n_grp:
-            lane_wait(1, s, 0)
-            for d in range(1, n_z):
-                lane_copy(1, s, 0, 0, d)
-            pair_copy(1, s, 0)
-    for sz in range(n_z):
-        for sg in range(1, n_grp):
-            lane_wait(0, sg, sz)
-            pair_copy(0, sg, sz)
-    for sg in range(n_grp):
-        for sz in range(1, n_z):
-            lane_wait(1, sg, sz) if sg or sz else None
-            pair_copy(1, sg, sz)
+    send_orbitals(0)
+
+    near = sorted(range(1, n_z), key=lambda s: (min(s, n_z - s), s))
+    for i in range(max(n_grp, n_z) - 1):
+        if i < n_z - 1:
+            lane_wait(0, 0, near[i])
+            for d in (1, 2):
+                start(lane_copy(0, 0, near[i], d, 0))
+            pair_copy(0, 0, near[i])
+        if i < n_grp - 1:
+            lane_wait(1, i + 1, 0)
+            pass_on(i + 1, 0)
+            pair_copy(1, i + 1, 0)
+    for c in range(1, len(cuts)):
+        send_orbitals(c)
+
+    for sz in [0] + near:
+        for d in (1, 2):
+            lane_wait(0, d, sz)
+            if d == 1 + sz % 2:
+                start(lane_copy(0, d, sz, 3 - d, 0))
+            pair_copy(0, d, sz)
+        if sz:
+            for sg in range(n_grp):
+                lane_wait(1, sg, sz)
+                pass_on(sg, sz)
+                pair_copy(1, sg, sz)
+    for sz in [0] + near:
+        lane_wait(0, 3, sz)
+        pair_copy(0, 3, sz)
     for copy in local:
         copy.wait()
-    for s in range(1, n_grp):
-        ref = table_v.at[grp_at(-s)]
+    for s in others:
+        ref = table_v.at[grp_at(s)]
         remote(ref, ref, list_send.at[s], list_recv.at[s], pair).wait_recv()
     to_scalar = pltpu.make_async_copy(table_v, table, table_sem.at[0])
     to_scalar.start()
     to_scalar.wait()
-    for k in range(2):
+
+    def pair_waits(k):
         for sg in range(n_grp):
             for sz in range(n_z):
                 pair_wait(k, sg, sz)
@@ -316,7 +337,7 @@
 
     def landing(c, s, r):
         begin, length = cuts[c]
-        rows = pl.ds(pl.multiple_of(grp_at(-s) * share + begin, ROW_TILE), length)
+        rows = pl.ds(pl.multiple_of(grp_at(s) * share + begin, ROW_TILE), length)
         return out.at[:, rows, pl.ds(r * tile_size, tile_size)]
 
     for c in range(len(cuts)):
@@ -324,19 +345,33 @@
             src, dst = in_piece(c, 0, r)
             pltpu.make_async_copy(src, dst, in_local.at[c, r]).wait()
             for s in range(1, n_grp):
-                ref = currents[c].at[grp_at(-s) * group_rows + r]
+                ref = currents[c].at[grp_at(s) * group_rows + r]
                 at = (c, s, r)
                 remote(ref, ref, in_send.at[at], in_recv.at[at], pair).wait_recv()
-        propagate(
-            currents[c], spread, sums, cosine, sine, table, n_grp, group_rows, slots
-        )
-        for r in range(group_rows):
-            for s in range(1, n_grp):
+        spread_group, double_group = stages(
+            currents[c], spread, sums, cosine, sine, table, group_rows, slots
+        )
+        if c == 0:
+            pair_waits(0)
+        lax.fori_loop(0, n_grp, spread_group, 0)
+        if c == 0:
+            pair_waits(1)
+
+        def step(_, carry):
+            lax.fori_loop(0, n_grp, double_group, 0)
+            lax.fori_loop(0, n_grp, spread_group, 0)
+            return carry
+
+        lax.fori_loop(0, STEPS - 1, step, 0)
+        for s in (3, 1, 2, 0):
+            double_group(grp_at(s), 0)
+            for r in range(group_rows):
                 src, dst = out_piece(c, s, r)
-                at = (c, s, r)
-                start(remote(src, dst, out_send.at[at], out_recv.at[at], device(s, 0)))
-            src, dst = out_piece(c, 0, r)
-            pltpu.make_async_copy(src, dst, out_local.at[c, r]).start()
+                if s == 0:
+                    pltpu.make_async_copy(src, dst, out_local.at[c, r]).start()
+                else:
+                    at = (c, s, r)
+                    start(remote(src, dst, out_send.at[at], out_recv.at[at], device(s, 0)))
     for c in range(len(cuts)):
         for r in range(group_rows):
             src, dst = out_piece(c, 0, r)
@@ -347,6 +382,8 @@
                 remote(ref, ref, out_send.at[at], out_recv.at[at], pair).wait_recv()
     for copy in sent:
         copy.wait_send()
+    for condition, copy in guarded:
+        pl.when(condition)(copy.wait_send)
 
 
 def chunk_cuts(share):
@@ -396,7 +433,7 @@
     return pl.pallas_call(
         functools.partial(kernel, n_grp, n_z, cuts, group_rows),
         out_shape=jax.ShapeDtypeStruct(orbitals.shape, orbitals.dtype),
-        in_specs=[pl.BlockSpec(memory_space=pl.ANY)] * 4,
+        in_specs=[pl.BlockSpec(memory_space=pltpu.HBM)] * 4,
         out_specs=pl.BlockSpec(memory_space=pl.ANY),
         scratch_shapes=scratch,
         compiler_params=pltpu.CompilerParams(
@@ -413,7 +450,7 @@
     fits = tile_bytes + 4 * orbitals.size * 2 < VMEM_LIMIT
     even = orbital_count % (n_grp * ROW_TILE) == 0 and tile_size % 128 == 0
     paired = n_col % 2 == 0 and slots == n_col and slots <= 128
-    if fits and even and paired and n_grp > 1 and n_col > 2:
+    if fits and even and paired and n_grp == 4 and n_col > 2:
         return exchange_plan(n_grp, n_col, orbitals, cosine_tiles, *rest)
     return gather_plan(orbitals, cosine_tiles, *rest)
 

time: 134 us -> 125 us (0.933)
  Pallas kernels: 128 us -> 119 us
    pallas_call x1, Pallas kernels: 128 us -> 119 us  [exchange_plan(): pl.pallas_call(functools.partial(kernel, n_grp, n_z, cuts, group_rows), o...]
where the time goes in v2:
time: 125 us
  Pallas kernels  119 us (95%)
  local copies, waits for them, and re-layouts  3.6 us (3%)
  other arithmetic  2.09 us (2%)
    pallas_call x1, Pallas kernels, exchange_plan(): pl.pallas_call(functools.partial(kernel, n_grp, n_z, cuts, group_rows), o...  119 us
    unnamed x5, local copies, waits for them, and re-layouts  3.56 us

profile of v2, /device:TPU:0, one launch (start us, length us, event | category | flops | bytes accessed | tf_op | source)
XLA Modules:
  0.0 124.7 jit_solution(14483762700721794873)
XLA Ops:
  0.0 0.9 select_reduce_fusion.2
  0.9 0.7 iota_add_fusion
  1.5 0.2 convert_reduce_fusion
  1.7 0.1 select_reduce_fusion
  1.9 0.1 add_compare_fusion
  1.9 0.2 convert_reduce_fusion.1
  2.2 0.0 copy-start
  2.2 0.9 copy-done
  3.1 0.0 copy-start.1
  3.1 0.9 copy-done.1
  4.0 118.9 %shard_map.64 = bf16[2,832,1024]{2,1,0:T(8,128)(2,1)S(1)} custom-call(bf16[2,832,1024]{2,1,0:T(8,128)(2,1)} %orb.1, bf16[1,256,256]{2,1,0:T(8,128)(2,1)S(1)} %copy-done, bf16[1,256,256]{2,1,0:T(8,128)(2,1)S(1)} %copy-done.1, s32[8,128]{1,0:T(8,128)S(1)} %pad.27.lists), custom_call_target="tpu_custom_call" | custom-call | tf_op jit(solution)/shard_map/pallas_call | solution.py:433
  122.9 1.8 %copy.8 = bf16[2,832,1024]{2,1,0:T(8,128)(2,1)} copy(bf16[2,832,1024]{2,1,0:T(8,128)(2,1)S(1)} %shard_map.64) | data formatting | bytes 6815744
  (6 shorter events, 0.1 us)
Async XLA Ops:
  2.2 0.9 copy-start
  3.1 0.9 copy-start.1

commit v3 on v2

--- a/solution.py
+++ b/solution.py
@@ -96,10 +96,8 @@
     return jnp.pad(jnp.stack(table), ((0, 8 - len(table)), (0, 0)))
 
 
-def dot_t(panel, tile):
-    return lax.dot_general(
-        panel, tile, (((1,), (1,)), ((), ())), preferred_element_type=jnp.float32
-    )
+def dot(panel, tile):
+    return jnp.dot(panel, tile, preferred_element_type=jnp.float32)
 
 
 def stages(current, spread, sums, cosine, sine, table, group_rows, slots):
@@ -114,7 +112,7 @@
         for k in range(slots):
             slot, source, keep = slot_values(g, k)
             panel = current[source].reshape(height, tile_size)
-            product = dot_t(panel, cosine[g, slot])
+            product = dot(panel, cosine[g, slot])
             total = product if k == 0 else product + total * keep
             sums[k, :height] = total
         for r in range(group_rows):
@@ -129,8 +127,8 @@
         for k in range(slots):
             slot, source, keep = slot_values(g, k)
             panel = spread[source, :height]
-            by_cosine = dot_t(panel, cosine[g, slot])
-            by_sine = dot_t(panel, sine[g, slot])
+            by_cosine = dot(panel, cosine[g, slot])
+            by_sine = dot(panel, sine[g, slot])
             product = jnp.concatenate(
                 [by_cosine[:length] + by_sine[length:], by_cosine[length:] - by_sine[:length]],
                 axis=0,
@@ -439,7 +437,7 @@
         compiler_params=pltpu.CompilerParams(
             collective_id=0, has_side_effects=True, vmem_limit_bytes=VMEM_LIMIT
         ),
-    )(orbitals, cosine_tiles, sine_tiles, lists)
+    )(orbitals, jnp.swapaxes(cosine_tiles, 1, 2), jnp.swapaxes(sine_tiles, 1, 2), lists)
 
 
 def on_device(n_grp, n_col, orbitals, cosine_tiles, *rest):

time: 125 us -> 122 us (0.976)
  Pallas kernels: 119 us -> 116 us
    pallas_call x1, Pallas kernels: 119 us -> 116 us  [exchange_plan(): pl.pallas_call(functools.partial(kernel, n_grp, n_z, cuts, group_rows), o...]
    unnamed x5 -> x3, local copies, waits for them, and re-layouts: 3.56 us -> 3.76 us
where the time goes in v3:
time: 122 us
  Pallas kernels  116 us (95%)
  local copies, waits for them, and re-layouts  3.8 us (3%)
  other arithmetic  2.09 us (2%)
    pallas_call x1, Pallas kernels, exchange_plan(): pl.pallas_call(functools.partial(kernel, n_grp, n_z, cuts, group_rows), o...  116 us
    unnamed x3, local copies, waits for them, and re-layouts  3.76 us

profile of v3, /device:TPU:0, one launch (start us, length us, event | category | flops | bytes accessed | tf_op | source)
XLA Modules:
  0.0 122.2 jit_solution(14711198578779170821)
XLA Ops:
  0.0 0.9 select_reduce_fusion.2
  0.9 0.7 iota_add_fusion
  1.5 0.2 convert_reduce_fusion
  1.7 0.1 select_reduce_fusion
  1.9 0.1 add_compare_fusion
  1.9 0.2 convert_reduce_fusion.1
  2.2 1.0 copy.9
  3.2 1.0 copy.10
  4.2 116.3 %shard_map.64 = bf16[2,832,1024]{2,1,0:T(8,128)(2,1)S(1)} custom-call(bf16[2,832,1024]{2,1,0:T(8,128)(2,1)} %orb.1, bf16[1,256,256]{2,1,0:T(8,128)(2,1)S(1)} %bitcast.13, bf16[1,256,256]{2,1,0:T(8,128)(2,1)S(1)} %bitcast.14, s32[8,128]{1,0:T(8,128)S(1)} %pad.27.lists), custom_call_target="tpu_custom_call" | custom-call | tf_op jit(solution)/shard_map/pallas_call | solution.py:431
  120.4 1.8 %copy.12 = bf16[2,832,1024]{2,1,0:T(8,128)(2,1)} copy(bf16[2,832,1024]{2,1,0:T(8,128)(2,1)S(1)} %shard_map.64) | data formatting | bytes 6815744
  (6 shorter events, 0.1 us)

commit v4 on v3

--- a/solution.py
+++ b/solution.py
@@ -176,7 +176,6 @@
     grp, col = lax.axis_index("grp"), lax.axis_index("col")
     z, core = col // 2, col % 2
     tiles = (cosine, sine)
-    own = (cos_in.at[0], sin_in.at[0])
 
     def grp_at(diff):
         return lax.rem(grp // 2 + diff // 2, 2) * 2 + lax.rem(grp + diff, 2)
@@ -209,6 +208,8 @@
     partners += [device(0, s) for s in range(1, n_z)] + [pair]
     for partner in partners:
         pl.semaphore_signal(barrier, inc=1, device_id=partner, device_id_type=MESH)
+    cosine[grp, col] = cos_in[0].T
+    sine[grp, col] = sin_in[0].T
     pl.semaphore_wait(barrier, len(partners))
 
     def tile_ref(k, tg, tz, lane):
@@ -216,9 +217,8 @@
 
     def lane_copy(k, tg, tz, dg, dz):
         dst = tile_ref(k, tg, tz, core)
-        src = own[k] if (tg, tz) == (0, 0) else dst
         at = (k, tg ^ dg, (tz + dz) % n_z)
-        return remote(src, dst, lane_send.at[at], lane_recv.at[at], device(dg, dz))
+        return remote(dst, dst, lane_send.at[at], lane_recv.at[at], device(dg, dz))
 
     def lane_wait(k, sg, sz):
         ref = tile_ref(k, sg, sz, core)
@@ -227,9 +227,8 @@
 
     def pair_copy(k, sg, sz):
         dst = tile_ref(k, sg, sz, core)
-        src = own[k] if (sg, sz) == (0, 0) else dst
         at = (k, sg, sz)
-        start(remote(src, dst, pair_send.at[at], pair_recv.at[at], pair))
+        start(remote(dst, dst, pair_send.at[at], pair_recv.at[at], pair))
 
     def pair_wait(k, sg, sz):
         ref = tile_ref(k, sg, sz, 1 - core)
@@ -258,11 +257,8 @@
     for s in range(1, n_z):
         start(lane_copy(0, 0, 0, 0, s))
     pass_on(0, 0)
-    local = [pltpu.make_async_copy(lists, table_v.at[grp], own_sem.at[2])]
-    for k in range(2):
-        local.append(pltpu.make_async_copy(own[k], tile_ref(k, 0, 0, core), own_sem.at[k]))
-    for copy in local:
-        copy.start()
+    own_lists = pltpu.make_async_copy(lists, table_v.at[grp], own_sem.at[0])
+    own_lists.start()
     for k in range(2):
         pair_copy(k, 0, 0)
     for s in (1, 2):
@@ -296,25 +292,32 @@
             lane_wait(1, i + 1, 0)
             pass_on(i + 1, 0)
             pair_copy(1, i + 1, 0)
-    for c in range(1, len(cuts)):
-        send_orbitals(c)
-
-    for sz in [0] + near:
+    def cosine_across(sz):
         for d in (1, 2):
             lane_wait(0, d, sz)
             if d == 1 + sz % 2:
                 start(lane_copy(0, d, sz, 3 - d, 0))
             pair_copy(0, d, sz)
-        if sz:
-            for sg in range(n_grp):
-                lane_wait(1, sg, sz)
-                pass_on(sg, sz)
-                pair_copy(1, sg, sz)
+
+    def sine_along(sz):
+        for sg in range(n_grp):
+            lane_wait(1, sg, sz)
+            pass_on(sg, sz)
+            pair_copy(1, sg, sz)
+
+    cosine_across(0)
+    for sz in near[:2]:
+        sine_along(sz)
+    for sz in near:
+        cosine_across(sz)
+    for c in range(1, len(cuts)):
+        send_orbitals(c)
+    for sz in near[2:]:
+        sine_along(sz)
     for sz in [0] + near:
         lane_wait(0, 3, sz)
         pair_copy(0, 3, sz)
-    for copy in local:
-        copy.wait()
+    own_lists.wait()
     for s in others:
         ref = table_v.at[grp_at(s)]
         remote(ref, ref, list_send.at[s], list_recv.at[s], pair).wait_recv()
@@ -420,7 +423,7 @@
         dma((2, n_grp, n_z)),
         dma((2, n_grp, n_z)),
         dma((2, n_grp, n_z)),
-        dma((3,)),
+        dma((1,)),
         dma(grid),
         dma(grid),
         dma((len(cuts), group_rows)),
@@ -431,13 +434,13 @@
     return pl.pallas_call(
         functools.partial(kernel, n_grp, n_z, cuts, group_rows),
         out_shape=jax.ShapeDtypeStruct(orbitals.shape, orbitals.dtype),
-        in_specs=[pl.BlockSpec(memory_space=pltpu.HBM)] * 4,
+        in_specs=[pl.BlockSpec(memory_space=space) for space in (pltpu.HBM, pltpu.VMEM, pltpu.VMEM, pltpu.HBM)],
         out_specs=pl.BlockSpec(memory_space=pl.ANY),
         scratch_shapes=scratch,
         compiler_params=pltpu.CompilerParams(
             collective_id=0, has_side_effects=True, vmem_limit_bytes=VMEM_LIMIT
         ),
-    )(orbitals, jnp.swapaxes(cosine_tiles, 1, 2), jnp.swapaxes(sine_tiles, 1, 2), lists)
+    )(orbitals, cosine_tiles, sine_tiles, lists)
 
 
 def on_device(n_grp, n_col, orbitals, cosine_tiles, *rest):

time: 122 us -> 123 us (level)
    unnamed x3 -> x5, local copies, waits for them, and re-layouts: 3.76 us -> 3.56 us
where the time goes in v4:
time: 123 us
  Pallas kernels  117 us (95%)
  local copies, waits for them, and re-layouts  3.6 us (3%)
  other arithmetic  2.09 us (2%)
    pallas_call x1, Pallas kernels, exchange_plan(): pl.pallas_call(functools.partial(kernel, n_grp, n_z, cuts, group_rows), o...  117 us
    unnamed x5, local copies, waits for them, and re-layouts  3.56 us

profile of v4, /device:TPU:0, one launch (start us, length us, event | category | flops | bytes accessed | tf_op | source)
XLA Modules:
  0.0 123.2 jit_solution(17441319379457372600)
XLA Ops:
  0.0 0.9 select_reduce_fusion.2
  0.9 0.7 iota_add_fusion
  1.5 0.2 convert_reduce_fusion
  1.7 0.1 select_reduce_fusion
  1.9 0.1 add_compare_fusion
  1.9 0.2 convert_reduce_fusion.1
  2.2 0.0 copy-start
  2.2 0.9 copy-done
  3.1 0.0 copy-start.1
  3.1 0.9 copy-done.1
  4.0 117.5 %shard_map.64 = bf16[2,832,1024]{2,1,0:T(8,128)(2,1)S(1)} custom-call(bf16[2,832,1024]{2,1,0:T(8,128)(2,1)} %orb.1, bf16[1,256,256]{2,1,0:T(8,128)(2,1)S(1)} %copy-done, bf16[1,256,256]{2,1,0:T(8,128)(2,1)S(1)} %copy-done.1, s32[8,128]{1,0:T(8,128)S(1)} %pad.27.lists), custom_call_target="tpu_custom_call" | custom-call | tf_op jit(solution)/shard_map/pallas_call | solution.py:434
  121.5 1.8 %copy.8 = bf16[2,832,1024]{2,1,0:T(8,128)(2,1)} copy(bf16[2,832,1024]{2,1,0:T(8,128)(2,1)S(1)} %shard_map.64) | data formatting | bytes 6815744
  (6 shorter events, 0.1 us)
Async XLA Ops:
  2.2 0.9 copy-start
  3.1 0.9 copy-start.1

commit v5 on v4

--- a/solution.py
+++ b/solution.py
@@ -100,7 +100,7 @@
     return jnp.dot(panel, tile, preferred_element_type=jnp.float32)
 
 
-def stages(current, spread, sums, cosine, sine, table, group_rows, slots):
+def stages(current, spread, sums, tiles, table, group_rows, slots):
     halves, length, tile_size = current.shape[1:]
     height = halves * length
 
@@ -112,27 +112,23 @@
         for k in range(slots):
             slot, source, keep = slot_values(g, k)
             panel = current[source].reshape(height, tile_size)
-            product = dot(panel, cosine[g, slot])
+            product = dot(panel, tiles[g, slot, :tile_size])
             total = product if k == 0 else product + total * keep
             sums[k, :height] = total
         for r in range(group_rows):
             used = table[g, 4, r].astype(jnp.float32)
-            spread[g * group_rows + r, :height] = (sums[table[g, 3, r], :height] * used).astype(
-                spread.dtype
-            )
+            rows = (sums[table[g, 3, r], :height] * used).astype(spread.dtype)
+            block = g * group_rows + r
+            spread[block, :height, :tile_size] = rows
+            spread[block, :length, tile_size:] = rows[length:]
+            spread[block, length:height, tile_size:] = -rows[:length]
         return carry
 
     def double_group(g, carry):
         total = None
         for k in range(slots):
             slot, source, keep = slot_values(g, k)
-            panel = spread[source, :height]
-            by_cosine = dot(panel, cosine[g, slot])
-            by_sine = dot(panel, sine[g, slot])
-            product = jnp.concatenate(
-                [by_cosine[:length] + by_sine[length:], by_cosine[length:] - by_sine[:length]],
-                axis=0,
-            )
+            product = dot(spread[source, :height], tiles[g, slot])
             total = product if k == 0 else product + total * keep
             sums[k, :height] = total
         for r in range(group_rows):
@@ -151,8 +147,7 @@
     (
         spread,
         sums,
-        cosine,
-        sine,
+        tiles,
         table_v,
         table,
         list_send,
@@ -170,12 +165,11 @@
         out_recv,
         out_local,
     ) = scratch[len(cuts) :]
-    tile_size = cosine.shape[-1]
-    slots = cosine.shape[1]
+    tile_size = tiles.shape[-1]
+    slots = tiles.shape[1]
     share = orb.shape[1] // n_grp
     grp, col = lax.axis_index("grp"), lax.axis_index("col")
     z, core = col // 2, col % 2
-    tiles = (cosine, sine)
 
     def grp_at(diff):
         return lax.rem(grp // 2 + diff // 2, 2) * 2 + lax.rem(grp + diff, 2)
@@ -208,12 +202,13 @@
     partners += [device(0, s) for s in range(1, n_z)] + [pair]
     for partner in partners:
         pl.semaphore_signal(barrier, inc=1, device_id=partner, device_id_type=MESH)
-    cosine[grp, col] = cos_in[0].T
-    sine[grp, col] = sin_in[0].T
+    tiles[grp, col, :tile_size] = cos_in[0].T
+    tiles[grp, col, tile_size:] = sin_in[0].T
     pl.semaphore_wait(barrier, len(partners))
 
     def tile_ref(k, tg, tz, lane):
-        return tiles[k].at[grp_at(tg), z_at(-tz) * 2 + lane]
+        place = grp_at(tg), z_at(-tz) * 2 + lane
+        return tiles.at[place[0], place[1], pl.ds(k * tile_size, tile_size)]
 
     def lane_copy(k, tg, tz, dg, dz):
         dst = tile_ref(k, tg, tz, core)
@@ -350,14 +345,12 @@
                 at = (c, s, r)
                 remote(ref, ref, in_send.at[at], in_recv.at[at], pair).wait_recv()
         spread_group, double_group = stages(
-            currents[c], spread, sums, cosine, sine, table, group_rows, slots
+            currents[c], spread, sums, tiles, table, group_rows, slots
         )
         if c == 0:
             pair_waits(0)
+            pair_waits(1)
         lax.fori_loop(0, n_grp, spread_group, 0)
-        if c == 0:
-            pair_waits(1)
-
         def step(_, carry):
             lax.fori_loop(0, n_grp, double_group, 0)
             lax.fori_loop(0, n_grp, spread_group, 0)
@@ -410,10 +403,9 @@
         pltpu.VMEM((blocks, halves, length, tile_size), orbitals.dtype) for _, length in cuts
     ]
     scratch += [
-        pltpu.VMEM((blocks, tallest, tile_size), jnp.bfloat16),
+        pltpu.VMEM((blocks, tallest, 2 * tile_size), jnp.bfloat16),
         pltpu.VMEM((slots, tallest, tile_size), jnp.float32),
-        pltpu.VMEM((n_grp, slots, tile_size, tile_size), cosine_tiles.dtype),
-        pltpu.VMEM((n_grp, slots, tile_size, tile_size), sine_tiles.dtype),
+        pltpu.VMEM((n_grp, slots, 2 * tile_size, tile_size), cosine_tiles.dtype),
         pltpu.VMEM((n_grp,) + lists.shape, jnp.int32),
         pltpu.SMEM((n_grp,) + lists.shape, jnp.int32),
         dma((n_grp,)),

time: 123 us -> 123 us (level)
  no operation moved by 1% of the time
where the time goes in v5:
time: 123 us
  Pallas kernels  117 us (95%)
  local copies, waits for them, and re-layouts  3.6 us (3%)
  other arithmetic  2.09 us (2%)
    pallas_call x1, Pallas kernels, exchange_plan(): pl.pallas_call(functools.partial(kernel, n_grp, n_z, cuts, group_rows), o...  117 us
    unnamed x5, local copies, waits for them, and re-layouts  3.56 us

profile of v5, /device:TPU:0, one launch (start us, length us, event | category | flops | bytes accessed | tf_op | source)
XLA Modules:
  0.0 123.2 jit_solution(85807125121537772)
XLA Ops:
  0.0 0.9 select_reduce_fusion.2
  0.9 0.7 iota_add_fusion
  1.5 0.2 convert_reduce_fusion
  1.7 0.1 select_reduce_fusion
  1.9 0.1 add_compare_fusion
  1.9 0.2 convert_reduce_fusion.1
  2.2 0.0 copy-start
  2.2 0.9 copy-done
  3.1 0.0 copy-start.1
  3.1 0.9 copy-done.1
  4.0 117.5 %shard_map.64 = bf16[2,832,1024]{2,1,0:T(8,128)(2,1)S(1)} custom-call(bf16[2,832,1024]{2,1,0:T(8,128)(2,1)} %orb.1, bf16[1,256,256]{2,1,0:T(8,128)(2,1)S(1)} %copy-done, bf16[1,256,256]{2,1,0:T(8,128)(2,1)S(1)} %copy-done.1, s32[8,128]{1,0:T(8,128)S(1)} %pad.27.lists), custom_call_target="tpu_custom_call" | custom-call | tf_op jit(solution)/shard_map/pallas_call | solution.py:426
  121.5 1.8 %copy.8 = bf16[2,832,1024]{2,1,0:T(8,128)(2,1)} copy(bf16[2,832,1024]{2,1,0:T(8,128)(2,1)S(1)} %shard_map.64) | data formatting | bytes 6815744
  (6 shorter events, 0.1 us)
Async XLA Ops:
  2.2 0.9 copy-start
  3.1 0.9 copy-start.1

commit v6 on v5

--- a/solution.py
+++ b/solution.py
@@ -11,7 +11,7 @@
 ROW_TILE = 16
 CHUNKS = 3
 MESH = pl.DeviceIdType.MESH
-VMEM_LIMIT = 48 * 2**20
+VMEM_LIMIT = 63 * 2**20
 
 
 def row_sums(product, rows_onehot):
@@ -287,6 +287,9 @@
             lane_wait(1, i + 1, 0)
             pass_on(i + 1, 0)
             pair_copy(1, i + 1, 0)
+    for c in range(1, len(cuts)):
+        send_orbitals(c)
+
     def cosine_across(sz):
         for d in (1, 2):
             lane_wait(0, d, sz)
@@ -305,8 +308,6 @@
         sine_along(sz)
     for sz in near:
         cosine_across(sz)
-    for c in range(1, len(cuts)):
-        send_orbitals(c)
     for sz in near[2:]:
         sine_along(sz)
     for sz in [0] + near:

time: 123 us -> 124 us (level)
    unnamed x5 -> x1, local copies, waits for them, and re-layouts: 3.56 us -> 4.05 us
where the time goes in v6:
time: 124 us
  Pallas kernels  117 us (94%)
  local copies, waits for them, and re-layouts  4.69 us (4%)
  other arithmetic  2.09 us (2%)
    pallas_call x1, Pallas kernels, exchange_plan(): pl.pallas_call(functools.partial(kernel, n_grp, n_z, cuts, group_rows), o...  117 us
    unnamed x1, local copies, waits for them, and re-layouts  4.05 us

profile of v6, /device:TPU:0, one launch (start us, length us, event | category | flops | bytes accessed | tf_op | source)
XLA Modules:
  0.0 124.3 jit_solution(7600948026273114198)
XLA Ops:
  0.0 0.9 select_reduce_fusion.2
  0.9 0.7 iota_add_fusion
  1.5 0.2 convert_reduce_fusion
  1.7 0.1 select_reduce_fusion
  1.9 0.1 add_compare_fusion
  1.9 0.2 convert_reduce_fusion.1
  2.1 0.6 pad.27.lists
  2.7 117.5 %shard_map.64 = bf16[2,832,1024]{2,1,0:T(8,128)(2,1)} custom-call(bf16[2,832,1024]{2,1,0:T(8,128)(2,1)} %orb.1, bf16[1,256,256]{2,1,0:T(8,128)(2,1)} %cos_in.1, bf16[1,256,256]{2,1,0:T(8,128)(2,1)} %sin_in.1, s32[8,128]{1,0:T(8,128)} %pad.27.lists), custom_call_target="tpu_custom_call" | custom-call | tf_op jit(solution)/shard_map/pallas_call | solution.py:427
  120.2 4.1 %copy.8 = bf16[2,832,1024]{2,1,0:T(8,128)(2,1)} copy(bf16[2,832,1024]{2,1,0:T(8,128)(2,1)} %shard_map.64) | data formatting | bytes 6815744
  (5 shorter events, 0.1 us)
